TPU v7x, 256 devices: a whole 4x4x8 slice. The times are simulated.
256 devices in a mesh: links: 64 (over x_hi, z, y), heads: 4 (over x_lo, core).
Axes of the slice: x: 4 (x_hi: 2, x_lo: 2; x = x_hi * 2 + x_lo), y: 4, z: 8, core: 2. Of those that a mesh axis runs over, the one named last changes fastest.
Arguments:
- queries: bfloat16 [65536, 512], P('links', 'heads'), may hold values from -6 to 6
- keys: bfloat16 [4096, 512], P('links', 'heads'), may hold values from -6 to 6
- values: bfloat16 [4096, 512], P('links', 'heads'), may hold values from -6 to 6
- attn: bfloat16 [65536, 512], P('links', 'heads'), may hold values from -6 to 6
- cotangent: bfloat16 [65536, 512], P('links', 'heads'), may hold values from -12 to 12
- out_weight: bfloat16 [512, 512], P('heads'), may hold values from -0.25 to 0.25
- lse: float32 [8, 65536], P('heads', 'links'), may hold values from 2 to 12
Outputs:
- query_grad: bfloat16 [65536, 512], P('links', 'heads')
- key_grad: bfloat16 [4096, 512], P('links', 'heads')
- value_grad: bfloat16 [4096, 512], P('links', 'heads')
All inputs are finite; a program needn't handle non-finite values.
Results may differ from a plain program's by a relative error of at most 0.028.
Values may be sent and summed in bfloat16 or wider, within the bound.
A program may use at most 64 MiB of HBM per device.

v0:
```python
import math

import jax
import jax.numpy as jnp
from jax import lax
from jax.sharding import PartitionSpec as P

DH = 64


def block_terms(query_rows, grad_rows, saved_lse, row_delta, key_block, value_block):
    scores = (
        jnp.einsum("qhd,khd->hqk", query_rows, key_block, preferred_element_type=jnp.float32)
        * 0.125
    )
    probs = jnp.exp(scores - saved_lse[:, :, None])
    dprob = jnp.einsum("qhd,khd->hqk", grad_rows, value_block, preferred_element_type=jnp.float32)
    score_grads = (0.125 * probs * (dprob - row_delta[:, :, None])).astype(jnp.bfloat16)
    return (probs.astype(jnp.bfloat16), score_grads)


def body(queries, keys, values, attn, cotangent, out_weight, lse):
    count_q = queries.shape[0]
    local_heads = queries.shape[1] // DH
    width = queries.shape[1]
    full_grad = lax.all_gather(cotangent, "heads", axis=1, tiled=True)
    d_attn = lax.dot_general(
        full_grad, out_weight, (((1,), (1,)), ((), ())), preferred_element_type=jnp.float32
    ).astype(jnp.bfloat16)
    query_rows = queries.reshape(count_q, local_heads, DH)
    grad_rows = d_attn.reshape(count_q, local_heads, DH)
    row_delta = jnp.sum(
        d_attn.astype(jnp.float32).reshape(count_q, local_heads, DH)
        * attn.reshape(count_q, local_heads, DH),
        -1,
    ).T
    zone_keys, zone_values = (
        lax.all_gather(keys, "links", axis=0, tiled=True),
        lax.all_gather(values, "links", axis=0, tiled=True),
    )
    count_k = zone_keys.shape[0]
    kblock = math.gcd(count_k, 1024)
    key_blocks = zone_keys.reshape(count_k // kblock, kblock, local_heads, DH)
    value_blocks = zone_values.reshape(count_k // kblock, kblock, local_heads, DH)
    start_grad = jnp.zeros((count_q, local_heads, DH), jnp.float32)

    def visit(query_acc, block_pair):
        key_block, value_block = block_pair
        soft, score_grads = block_terms(
            query_rows, grad_rows, lse, row_delta, key_block, value_block
        )
        query_acc = query_acc + jnp.einsum(
            "hqk,khd->qhd", score_grads, key_block, preferred_element_type=jnp.float32
        )
        key_part = jnp.einsum(
            "hqk,qhd->khd", score_grads, query_rows, preferred_element_type=jnp.float32
        )
        value_part = jnp.einsum("hqk,qhd->khd", soft, grad_rows, preferred_element_type=jnp.float32)
        joined = jnp.concatenate(
            [key_part.reshape(kblock, width), value_part.reshape(kblock, width)], 1
        )
        return (query_acc, joined)

    query_acc, joined_parts = lax.scan(visit, start_grad, (key_blocks, value_blocks))
    terms = joined_parts.reshape(count_k, 2 * width)
    owned = lax.psum_scatter(terms, "links", scatter_dimension=0, tiled=True)
    query_grad = query_acc.reshape(count_q, width).astype(jnp.bfloat16)
    key_grad = owned[:, :width].astype(jnp.bfloat16)
    value_grad = owned[:, width:].astype(jnp.bfloat16)
    return (query_grad, key_grad, value_grad)


def solution(mesh):
    in_specs = (
        P("links", "heads"),
        P("links", "heads"),
        P("links", "heads"),
        P("links", "heads"),
        P("links", "heads"),
        P("heads", None),
        P("heads", "links"),
    )
    out_specs = (P("links", "heads"), P("links", "heads"), P("links", "heads"))
    return jax.shard_map(body, mesh=mesh, in_specs=in_specs, out_specs=out_specs, check_vma=False)
```

profile of v0, /device:TPU:2, one launch (start us, length us, event | category | flops | bytes accessed | tf_op | source)
XLA Modules:
  0.0 700.8 jit_solution(9120771481702425383)
XLA Ops:
  7.2 0.7 all-gather.8.cloned.1.call-update
  8.0 0.7 all-gather.6.cloned.1.call-update
  8.7 0.7 all-gather.4.cloned.1.call-update
  9.5 1.1 copy.15
  10.6 1.1 copy.17
  11.7 24.5 %all-gather.8.cloned.1.call-done = bf16[1024,512]{1,0:T(8,128)(2,1)} async-done(((bf16[1024,128]{1,0:T(8,128)(2,1)}), bf16[1024,512]{1,0:T(8,128)(2,1)}) %all-gather.8.cloned.1.call-update) | async-done | bytes 1048592 | tf_op jit(solution)/shard_map/all_gather | solution.py:26
  36.1 1.7 bitcast_reduce_fusion
  37.9 116.8 %all-gather.6.cloned.1.call-done = bf16[4096,128]{1,0:T(8,128)(2,1)} async-done(((bf16[64,128]{1,0:T(8,128)(2,1)}), bf16[4096,128]{1,0:T(8,128)(2,1)}) %all-gather.6.cloned.1.call-update) | async-done | bytes 1048592 | tf_op jit(solution)/shard_map/all_gather | solution.py:39
  154.6 3.9 reshape.43
  158.5 3.5 copy.19
  162.0 107.5 %all-gather.4.cloned.1.call-done = bf16[4096,128]{1,0:T(8,128)(2,1)} async-done(((bf16[64,128]{1,0:T(8,128)(2,1)}), bf16[4096,128]{1,0:T(8,128)(2,1)}) %all-gather.4.cloned.1.call-update) | async-done | bytes 1048592 | tf_op jit(solution)/shard_map/all_gather | solution.py:38
  269.5 3.9 reshape.42
  273.4 3.5 copy.18
  277.0 48.9 %while.13 = (s32[]{:T(128)}, f32[1024,2,64]{0,2,1:T(8,128)S(1)}, f32[4,1024,256]{2,1,0:T(8,128)}, bf16[4,1024,2,64]{1,3,2,0:T(8,128)(2,1)}, bf16[1024,2,64]{0,2,...) while((s32[]{:T(128)}, f32[1024,2,64]{0,2,1:T(8,128)S(1)}, ...), condition=%wide.region_2.3_spmd.clone, body=%wide.region_1.2_spmd.clone.sunk | while | flops 1361575936 | bytes 47997068 | solution.py:64
  277.0 2.2 fusion.49
  279.2 1.6 fusion.51
  280.8 3.6 multiply_convert_fusion.2
  284.4 1.9 fusion.50
  286.3 1.4 fusion.52
  287.7 0.1 maximum_bitcast_fusion.2
  287.8 0.3 copy.30
  288.1 1.0 constant_dynamic-update-slice_fusion.2
  289.2 2.2 fusion.49
  291.4 1.6 fusion.51
  293.0 3.6 multiply_convert_fusion.2
  296.6 1.9 fusion.50
  298.5 1.4 fusion.52
  299.9 0.1 maximum_bitcast_fusion.2
  300.0 0.3 copy.30
  300.3 1.1 constant_dynamic-update-slice_fusion.2
  301.4 2.2 fusion.49
  303.6 1.6 fusion.51
  305.2 3.6 multiply_convert_fusion.2
  308.8 1.9 fusion.50
  310.7 1.4 fusion.52
  312.2 0.3 copy.30
  312.5 1.1 constant_dynamic-update-slice_fusion.2
  313.6 2.2 fusion.49
  315.8 1.6 fusion.51
  317.4 3.6 multiply_convert_fusion.2
  321.0 1.9 fusion.50
  322.9 1.4 fusion.52
  324.4 0.3 copy.30
  324.8 1.1 constant_dynamic-update-slice_fusion.2
  325.9 0.8 copy.21
  326.7 366.0 %reduce-scatter.2.cloned.1.call-done = f32[64,256]{1,0:T(8,128)} async-done(((f32[4096,256]{1,0:T(8,128)}), f32[64,256]{1,0:T(8,128)}) %reduce-scatter.2.cloned.1.call-update) | async-done | bytes 65552 | tf_op jit(solution)/shard_map/reduce_scatter | solution.py:66
  692.8 0.8 convert.4
  693.6 0.6 fusion.15
  (14 shorter events, 0.4 us)
Async XLA Ops:
  7.2 29.0 %copy-start = (bf16[128,512]{1,0:T(8,128)(2,1)S(1)}, bf16[128,512]{1,0:T(8,128)(2,1)}, u32[]{:S(2)}) copy-start(bf16[128,512]{1,0:T(8,128)(2,1)} %param.14) | copy-start | bytes 393220
  7.2 269.8 %copy-start.1 = (f32[2,1024]{1,0:T(2,128)S(1)}, f32[2,1024]{1,0:T(2,128)}, u32[]{:S(2)}) copy-start(f32[2,1024]{1,0:T(2,128)} %param.15) | copy-start | bytes 24580
  7.2 29.0 %all-gather.8.cloned.1.call-start = ((), (), s32[]{:S(2)}) async-start(), calls=%async_computation.3 | async-start | bytes 1310720 | tf_op jit(solution)/shard_map/all_gather | solution.py:26
  7.9 146.7 %all-gather.6.cloned.1.call-start = ((), (), s32[]{:S(2)}) async-start(), calls=%async_computation.2 | async-start | bytes 1064960 | tf_op jit(solution)/shard_map/all_gather | solution.py:39
  8.7 260.9 %all-gather.4.cloned.1.call-start = ((), (), s32[]{:S(2)}) async-start(), calls=%async_computation.1 | async-start | bytes 1064960 | tf_op jit(solution)/shard_map/all_gather | solution.py:38
  9.4 683.4 %reduce-scatter.2.cloned.1.call-start = ((), (), s32[]{:S(2)}) async-start(), calls=%async_computation.4 | async-start | bytes 4259840 | tf_op jit(solution)/shard_map/reduce_scatter | solution.py:66
Sparse Core Ops, SparseCore 0:
  9.8 26.2 all-gather.7
  39.9 114.7 all-gather.5
  158.4 111.1 all-gather.3
  326.0 366.7 reduce-scatter.1
where the time goes:
time: 701 us
  waiting for transfers between devices  617 us (88%)
  matrix products  44.6 us (6%)
  local copies, waits for them, and re-layouts  24 us (3%)
  between operations  13.8 us (2%)
    reduce_scatter x1, waiting for transfers between devices, body(): owned = lax.psum_scatter(terms, 'links', scatter_dimension=0, tiled=True)  366 us
    all_gather x1, waiting for transfers between devices, body(): lax.all_gather(values, 'links', axis=0, tiled=True)  117 us
    all_gather x1, waiting for transfers between devices, body(): lax.all_gather(keys, 'links', axis=0, tiled=True)  107 us
    all_gather x1, waiting for transfers between devices, body(): full_grad = lax.all_gather(cotangent, 'heads', axis=1, tiled=True)  24.5 us
    dot_general x4, matrix products, block_terms(): jnp.einsum('qhd,khd->hqk', grad_rows, value_block, preferred_element_type...  14.5 us
  transfers between devices with their start and end apart: 4, of which 4 were waited for; matrix products, arithmetic and copies ran while one was open for 2% of the time, Pallas kernels for 0%

commit v1 on v0

v1 whole, which is shorter than its diff:
```python
import jax
import jax.numpy as jnp
from jax import lax
from jax.experimental import pallas as pl
from jax.experimental.pallas import tpu as pltpu
from jax.sharding import PartitionSpec as P

F32, BF = jnp.float32, jnp.bfloat16
MESH = pl.DeviceIdType.MESH
LOG2E = 1.4426950408889634

XH, NZD, NYD = 2, 8, 4
ROWS = 1024
SHARD = 64
WIDTH = 128
DH = 64
CHUNK = 256
AUG = 256
ORDER = (4, 3, 5, 2, 6, 1, 7, 0)
PLACE = {r: i for i, r in enumerate(ORDER)}
YSTEP = (0, 1, 3, 2)
PIECES = 4
PROWS = ROWS // PIECES


def mm(a, b):
    return jnp.dot(a, b, preferred_element_type=F32)


def three(row):
    a = row.astype(BF).astype(F32)
    b = (row - a).astype(BF).astype(F32)
    return [a, b, row - a - b]


def aug_rows(row):
    return jnp.concatenate([*three(row), jnp.zeros((13, row.shape[1]), F32)], 0).astype(BF)


def kernel(
    q_in, k_in, v_in, attn_in, cot_in, w_in, lse_in,
    dq_out, dk_out, dv_out,
    cot, qa, da, lse2, delta2, qx, dx, kv, acc, psend, precv, zsend, zrecv, p_t, s_t, dq_t, dqs, dqr,
    cot_ss, cot_rs, z_ss, z_rs, y_ss, y_rs, x_ss, x_rs, r_ss, r_rs, g_ss, g_rs, dq_ss, dq_rs,
):
    link, head = lax.axis_index("links"), lax.axis_index("heads")
    xh, z, y = link // (NZD * NYD), (link // NYD) % NZD, link % NYD
    xl, core = head // 2, head % 2

    def at(dxh=0, dz=0, dy=0, dxl=0, dc=0):
        return (
            ((xh + dxh) % XH) * (NZD * NYD) + ((z + dz) % NZD) * NYD + (y + dy) % NYD,
            ((xl + dxl) % 2) * 2 + (core + dc) % 2,
        )

    def copy(src, dst, ss, rs, to):
        return pltpu.make_async_remote_copy(
            src_ref=src, dst_ref=dst, send_sem=ss, recv_sem=rs, device_id=to, device_id_type=MESH
        )

    def piece(i):
        return pl.ds(i * PROWS, PROWS)

    across = [
        copy(cot_in.at[piece(i)], cot.at[2, piece(i)], cot_ss.at[0, i], cot_rs.at[0, i], at(dxl=1))
        for i in range(PIECES)
    ]
    beside = copy(cot_in, cot.at[1], cot_ss.at[1, 0], cot_rs.at[1, 0], at(dc=1))
    onward = [
        copy(cot.at[2, piece(i)], cot.at[3, piece(i)], cot_ss.at[2, i], cot_rs.at[2, i], at(dc=1))
        for i in range(PIECES)
    ]
    shard = kv.at[0, PLACE[0]]
    along_z = {
        r: copy(shard, kv.at[0, PLACE[(NZD - r) % NZD]], z_ss.at[r], z_rs.at[r], at(dz=r))
        for r in (4, 3, 5, 2, 6, 1, 7)
    }
    along_y = {
        k: copy(kv.at[0], kv.at[k], y_ss.at[k], y_rs.at[k], at(dy=-YSTEP[k])) for k in (1, 2, 3)
    }
    swap_q = copy(q_in, qa.at[1], x_ss.at[0], x_rs.at[0], at(dxh=1))
    swap_l = copy(lse_in, lse2.at[1], x_ss.at[1], x_rs.at[1], at(dxh=1))
    swap_d = copy(delta2.at[0], delta2.at[1], x_ss.at[2], x_rs.at[2], at(dxh=1))
    swap_a = copy(da.at[0], da.at[1], x_ss.at[3], x_rs.at[3], at(dxh=1))
    back_y = {
        k: copy(psend.at[k - 1], precv.at[k - 1], r_ss.at[k], r_rs.at[k], at(dy=YSTEP[k]))
        for k in (1, 2, 3)
    }
    back_z = {
        r: copy(zsend.at[PLACE[r]], zrecv.at[r - 1], g_ss.at[r], g_rs.at[r], at(dz=r))
        for r in (4, 3, 5, 2, 6, 1, 7)
    }
    back_q = copy(dqs, dqr, dq_ss.at[0], dq_rs.at[0], at(dxh=1))

    for c in across:
        c.start()
    beside.start()
    kv[0, PLACE[0], 0] = k_in[...]
    kv[0, PLACE[0], 1] = v_in[...]
    for c in along_z.values():
        c.start()

    qa[0] = q_in[...]
    lse2[0] = lse_in[...]
    qx[...] = jnp.zeros_like(qx)
    dx[...] = jnp.zeros_like(dx)
    dq_t[...] = jnp.zeros_like(dq_t)
    acc[...] = jnp.zeros_like(acc)

    def widen_q(half):
        turned = qa[half].T
        for h in range(2):
            own = slice(DH * h, DH * h + DH)
            qx[half, h, own, :] = (turned[own].astype(F32) * 0.125).astype(BF)
            qx[half, h, WIDTH : WIDTH + 16, :] = aug_rows(lse2[half, h : h + 1, :])

    def widen_d(half, turned):
        for h in range(2):
            own = slice(DH * h, DH * h + DH)
            dx[half, h, own, :] = turned[own]
            dx[half, h, WIDTH : WIDTH + 16, :] = aug_rows(delta2[half, h : h + 1, :])

    widen_q(0)
    attn_t = attn_in[...].T

    for i in range(PIECES):
        across[i].wait_recv()
        onward[i].start()
    swap_q.start()
    swap_l.start()
    for c in along_z.values():
        c.wait_recv()
    for k in (1, 2, 3):
        along_y[k].start()
    beside.wait_recv()

    def block(dxl, dc):
        which = ((xl + dxl) % 2) * 2 + (core + dc) % 2
        return w_in[:, pl.ds(pl.multiple_of(which * WIDTH, WIDTH), WIDTH)]

    weight = jnp.concatenate([block(0, 0), block(0, 1), block(1, 0), block(1, 1)], 1)
    for i in range(PIECES):
        onward[i].wait_recv()
        rows = pl.ds(i * PROWS, PROWS)
        wide = jnp.concatenate([cot_in[rows, :], cot[1, rows], cot[2, rows], cot[3, rows]], 1)
        da[0, rows] = lax.dot_general(
            wide, weight, (((1,), (1,)), ((), ())), preferred_element_type=F32
        ).astype(BF)
    swap_a.start()
    turned = da[0].T
    product = turned.astype(F32) * attn_t.astype(F32)
    for h in range(2):
        delta2[0, h : h + 1, :] = jnp.sum(product[DH * h : DH * h + DH], axis=0, keepdims=True)
    swap_d.start()
    widen_d(0, turned)

    lane = lax.broadcasted_iota(jnp.int32, (CHUNK, WIDTH), 1)
    minus = jnp.where(lane < 3, -1.0, 0.0).astype(BF)
    left = lane < DH
    tile = 256

    def step(u, _):
        half, m = u // 8, u % 8
        k = half * 3 + (1 - 2 * half) * (m // 2)
        first = (m % 2) * 4

        for cls in (1, 2, 3):

            @pl.when(u == 2 * cls)
            def _():
                along_y[cls].wait_recv()

        @pl.when(u == 8)
        def _():
            swap_q.wait_recv()
            swap_l.wait_recv()
            swap_d.wait_recv()
            swap_a.wait_recv()
            widen_q(1)
            widen_d(1, da[1].T)

        places = pl.ds(first, 4)
        keys = kv[k, places, 0].reshape(CHUNK, WIDTH)
        values = kv[k, places, 1].reshape(CHUNK, WIDTH)
        wide_k = jnp.concatenate([keys, minus], 1)
        wide_v = jnp.concatenate([values, minus], 1)
        keys_t = keys.T
        outs = []
        for h in range(2):
            for j in range(ROWS // tile):
                cols = slice(j * tile, (j + 1) * tile)
                scores = mm(wide_k, qx[half, h, :, cols])
                moved = mm(wide_v, dx[half, h, :, cols])
                probs = jnp.exp2(scores * LOG2E)
                p_t[h, :, cols] = probs.astype(BF)
                s_t[h, :, cols] = (probs * moved).astype(BF)
            own = slice(DH * h, DH * h + DH)
            outs.append((mm(s_t[h], qa[half]), mm(p_t[h], da[half])))
            dq_t[half, own, :] += mm(keys_t[own], s_t[h])
        grad_k = jnp.where(left, outs[0][0], outs[1][0]) * 0.125
        grad_v = jnp.where(left, outs[0][1], outs[1][1])
        acc[k, places, 0] += grad_k.reshape(4, SHARD, WIDTH)
        acc[k, places, 1] += grad_v.reshape(4, SHARD, WIDTH)

        for cls in (3, 2, 1):

            @pl.when(u == 15 - 2 * cls)
            def _():
                psend[cls - 1] = acc[cls].astype(BF)
                back_y[cls].start()

        return 0

    lax.fori_loop(0, 16, step, 0)

    dqs[...] = (dq_t[1].T * 0.125).astype(BF)
    back_q.start()
    for cls in (3, 2, 1):
        back_y[cls].wait_recv()
    line = acc[0]
    for cls in (3, 2, 1):
        line = line + precv[cls - 1].astype(F32)
    acc[0] = line
    zsend[...] = line.astype(BF)
    for c in back_z.values():
        c.start()
    mine = (dq_t[0].T * 0.125).astype(F32)
    total = acc[0, PLACE[0]]
    for r, c in back_z.items():
        c.wait_recv()
        total = total + zrecv[r - 1].astype(F32)
    dk_out[...] = total[0].astype(BF)
    dv_out[...] = total[1].astype(BF)
    back_q.wait_recv()
    dq_out[...] = (mine + dqr[...].astype(F32)).astype(BF)

    for c in (
        *across, beside, *onward, *along_z.values(), *along_y.values(), swap_q, swap_l, swap_d, swap_a,
        *back_y.values(), *back_z.values(), back_q,
    ):
        c.wait_send()


def body(queries, keys, values, attn, cotangent, out_weight, lse):
    vmem = pl.BlockSpec(memory_space=pltpu.VMEM)
    dma = pltpu.SemaphoreType.DMA
    return pl.pallas_call(
        kernel,
        out_shape=[
            jax.ShapeDtypeStruct((ROWS, WIDTH), BF),
            jax.ShapeDtypeStruct((SHARD, WIDTH), BF),
            jax.ShapeDtypeStruct((SHARD, WIDTH), BF),
        ],
        in_specs=[vmem] * 7,
        out_specs=[vmem] * 3,
        scratch_shapes=[
            pltpu.VMEM((4, ROWS, WIDTH), BF),
            pltpu.VMEM((2, ROWS, WIDTH), BF),
            pltpu.VMEM((2, ROWS, WIDTH), BF),
            pltpu.VMEM((2, 2, ROWS), F32),
            pltpu.VMEM((2, 2, ROWS), F32),
            pltpu.VMEM((2, 2, AUG, ROWS), BF),
            pltpu.VMEM((2, 2, AUG, ROWS), BF),
            pltpu.VMEM((4, NZD, 2, SHARD, WIDTH), BF),
            pltpu.VMEM((4, NZD, 2, SHARD, WIDTH), F32),
            pltpu.VMEM((3, NZD, 2, SHARD, WIDTH), BF),
            pltpu.VMEM((3, NZD, 2, SHARD, WIDTH), BF),
            pltpu.VMEM((NZD, 2, SHARD, WIDTH), BF),
            pltpu.VMEM((NZD - 1, 2, SHARD, WIDTH), BF),
            pltpu.VMEM((2, CHUNK, ROWS), BF),
            pltpu.VMEM((2, CHUNK, ROWS), BF),
            pltpu.VMEM((2, WIDTH, ROWS), F32),
            pltpu.VMEM((ROWS, WIDTH), BF),
            pltpu.VMEM((ROWS, WIDTH), BF),
            dma((3, PIECES)), dma((3, PIECES)),
            dma((NZD,)), dma((NZD,)),
            dma((4,)), dma((4,)),
            dma((4,)), dma((4,)),
            dma((4,)), dma((4,)),
            dma((NZD,)), dma((NZD,)),
            dma((1,)), dma((1,)),
        ],
        compiler_params=pltpu.CompilerParams(
            has_side_effects=True, vmem_limit_bytes=48 * 2**20
        ),
        cost_estimate=pl.CostEstimate(
            flops=11 * 10**9, bytes_accessed=3 * 2**20, transcendentals=2**23
        ),
    )(queries, keys, values, attn, cotangent, out_weight, lse)


def solution(mesh):
    in_specs = (
        P("links", "heads"),
        P("links", "heads"),
        P("links", "heads"),
        P("links", "heads"),
        P("links", "heads"),
        P("heads", None),
        P("heads", "links"),
    )
    out_specs = (P("links", "heads"), P("links", "heads"), P("links", "heads"))
    return jax.shard_map(body, mesh=mesh, in_specs=in_specs, out_specs=out_specs, check_vma=False)
```

time: 701 us -> 75.1 us (0.11)
  waiting for transfers between devices: 617 us -> 0 us
  Pallas kernels: 0 us -> 66.3 us
  matrix products: 44.6 us -> 0 us
  local copies, waits for them, and re-layouts: 24 us -> 7.79 us
  between operations: 13.8 us -> 0.66 us
    reduce_scatter x1 -> x0, waiting for transfers between devices: 366 us -> none  [body(): owned = lax.psum_scatter(terms, 'links', scatter_dimension=0, tiled=True)]
    all_gather x3 -> x0, waiting for transfers between devices: 249 us -> none  [the longest x1 117 us: body(): lax.all_gather(values, 'links', axis=0, tiled=True)]
    pallas_call x0 -> x1, Pallas kernels: none -> 66.3 us  [body(): pl.pallas_call(kernel, out_shape=[jax.ShapeDtypeStruct((ROWS, WIDTH), BF)...]
    dot_general x21 -> x0, matrix products: 44.6 us -> none  [the longest x4 14.5 us: block_terms(): jnp.einsum('qhd,khd->hqk', grad_rows, value_block, preferred_element_type...]
    reshape x2 -> x0, local copies, waits for them, and re-layouts: 7.74 us -> none  [the longest x1 3.87 us: body(): zone_values.reshape(count_k // kblock, kblock, local_heads, DH)]
  transfers between devices with their start and end apart: 4 -> 0, of which waited for: 4 -> 0; matrix products, arithmetic and copies ran while one was open for 2% -> 0% of each run, Pallas kernels for 0% -> 0%
where the time goes in v1:
time: 75.1 us; the launch traced here: 74.7 us
  Pallas kernels  66.3 us (88%)
  local copies, waits for them, and re-layouts  7.79 us (10%)
    pallas_call x1, Pallas kernels, body(): pl.pallas_call(kernel, out_shape=[jax.ShapeDtypeStruct((ROWS, WIDTH), BF)...  66.3 us
    unnamed x17, local copies, waits for them, and re-layouts  7.79 us

profile of v1, /device:TPU:2, one launch (start us, length us, event | category | flops | bytes accessed | tf_op | source)
XLA Modules:
  0.0 74.7 jit_solution(11550787496085887897)
XLA Ops:
  0.6 0.0 copy-start
  0.6 0.9 %copy-done = bf16[1024,128]{1,0:T(8,128)(2,1)S(1)} copy-done((bf16[1024,128]{1,0:T(8,128)(2,1)S(1)}, bf16[1024,128]{1,0:T(8,128)(2,1)}, u32[]{:S(2)}) %copy-start) | copy-done | bytes 262168
  1.6 0.0 copy-start.1
  1.6 0.9 %copy-done.1 = bf16[1024,128]{1,0:T(8,128)(2,1)S(1)} copy-done((bf16[1024,128]{1,0:T(8,128)(2,1)S(1)}, bf16[1024,128]{1,0:T(8,128)(2,1)}, u32[]{:S(2)}) %copy-start.1) | copy-done | bytes 262168
  2.5 0.0 copy-start.2
  2.5 0.9 %copy-done.2 = bf16[1024,128]{1,0:T(8,128)(2,1)S(1)} copy-done((bf16[1024,128]{1,0:T(8,128)(2,1)S(1)}, bf16[1024,128]{1,0:T(8,128)(2,1)}, u32[]{:S(2)}) %copy-start.2) | copy-done | bytes 262168
  3.5 0.0 copy-start.3
  3.5 0.9 %copy-done.3 = bf16[128,512]{1,0:T(8,128)(2,1)S(1)} copy-done((bf16[128,512]{1,0:T(8,128)(2,1)S(1)}, bf16[128,512]{1,0:T(8,128)(2,1)}, u32[]{:S(2)}) %copy-start.3) | copy-done | bytes 131096
  4.4 0.0 copy-start.4
  4.4 0.7 copy-done.4
  5.1 0.0 copy-start.5
  5.1 0.7 copy-done.5
  5.8 0.0 copy-start.6
  5.8 0.7 copy-done.6
  6.5 66.3 %shard_map.94 = (bf16[1024,128]{1,0:T(8,128)(2,1)S(1)}, bf16[64,128]{1,0:T(8,128)(2,1)S(1)}, bf16[64,128]{1,0:T(8,128)(2,1)S(1)}) custom-call(bf16[1024,128]{1,0:T(8,128)(2,1)S(1)} %copy-done, bf16[64,128]{1,0:T(8,128)(2,1)S(1)} %copy-done.4, bf16[64,128]{1,0:T(8,128)(2,1)S(1)} %copy-done.5, bf16[1024,128]{1,0:T(8,128)(2,1)S(1)} %copy-done.1, ...), custom_call_target="tpu_custom_call" | custom-call | flops 11000000512 | bytes 3145728 | tf_op jit(solution)/shard_map/pallas_call | solution.py:247
  72.8 0.7 copy.13
  73.5 0.6 copy.14
  74.1 0.6 copy.15
Async XLA Ops:
  0.6 1.0 %copy-start = (bf16[1024,128]{1,0:T(8,128)(2,1)S(1)}, bf16[1024,128]{1,0:T(8,128)(2,1)}, u32[]{:S(2)}) copy-start(bf16[1024,128]{1,0:T(8,128)(2,1)} %q_in.1) | copy-start | bytes 786436
  1.6 0.9 %copy-start.1 = (bf16[1024,128]{1,0:T(8,128)(2,1)S(1)}, bf16[1024,128]{1,0:T(8,128)(2,1)}, u32[]{:S(2)}) copy-start(bf16[1024,128]{1,0:T(8,128)(2,1)} %attn_in.1) | copy-start | bytes 786436
  2.5 0.9 %copy-start.2 = (bf16[1024,128]{1,0:T(8,128)(2,1)S(1)}, bf16[1024,128]{1,0:T(8,128)(2,1)}, u32[]{:S(2)}) copy-start(bf16[1024,128]{1,0:T(8,128)(2,1)} %cot_in.1) | copy-start | bytes 786436
  3.5 0.9 %copy-start.3 = (bf16[128,512]{1,0:T(8,128)(2,1)S(1)}, bf16[128,512]{1,0:T(8,128)(2,1)}, u32[]{:S(2)}) copy-start(bf16[128,512]{1,0:T(8,128)(2,1)} %w_in.1) | copy-start | bytes 393220
  4.4 0.7 copy-start.4
  5.1 0.7 copy-start.5
  5.8 0.7 copy-start.6

commit v2 on v1

--- a/solution.py
+++ b/solution.py
@@ -19,6 +19,14 @@
 ORDER = (4, 3, 5, 2, 6, 1, 7, 0)
 PLACE = {r: i for i, r in enumerate(ORDER)}
 YSTEP = (0, 1, 3, 2)
+FAR, NEAR = 0, 1
+UNITS = (
+    (0, 0, FAR), (0, 1, NEAR), (0, 2, NEAR), (0, 1, FAR), (0, 2, FAR), (0, 3, NEAR), (0, 3, FAR),
+    (1, 3, FAR), (1, 1, FAR), (1, 2, FAR), (1, 0, FAR), (1, 3, NEAR), (1, 1, NEAR), (1, 2, NEAR), (1, 0, NEAR),
+    (0, 0, NEAR),
+)
+TURN = {unit: i for i, unit in enumerate(UNITS)}
+HALF_R = {FAR: (4, 3, 5, 2), NEAR: (6, 1, 7)}
 PIECES = 4
 PROWS = ROWS // PIECES
 
@@ -40,7 +48,7 @@
 def kernel(
     q_in, k_in, v_in, attn_in, cot_in, w_in, lse_in,
     dq_out, dk_out, dv_out,
-    cot, qa, da, lse2, delta2, qx, dx, kv, acc, psend, precv, zsend, zrecv, p_t, s_t, dq_t, dqs, dqr,
+    attn, w, in_sem, cot, qa, da, lse2, delta2, qx, dx, kv, acc, psend, precv, zsend, zrecv, p_t, s_t, dq_t, dqs, dqr,
     cot_ss, cot_rs, z_ss, z_rs, y_ss, y_rs, x_ss, x_rs, r_ss, r_rs, g_ss, g_rs, dq_ss, dq_rs,
 ):
     link, head = lax.axis_index("links"), lax.axis_index("heads")
@@ -60,6 +68,22 @@
 
     def piece(i):
         return pl.ds(i * PROWS, PROWS)
+
+    def half_at(p):
+        return pl.ds(p * 4, 4)
+
+    partners = [at(dz=r) for r in range(1, NZD)] + [at(dy=r) for r in range(1, NYD)]
+    partners += [at(dxh=1), at(dxl=1), at(dc=1)]
+    barrier = pltpu.get_barrier_semaphore()
+    for to in partners:
+        pl.semaphore_signal(barrier, inc=1, device_id=to, device_id_type=MESH)
+    places = (
+        (k_in, kv.at[0, PLACE[0], 0]), (v_in, kv.at[0, PLACE[0], 1]), (q_in, qa.at[0]),
+        (attn_in, attn), (lse_in, lse2.at[0]), (w_in, w), (cot_in, cot.at[0]),
+    )
+    fetch = [pltpu.make_async_copy(src, dst, in_sem.at[i]) for i, (src, dst) in enumerate(places)]
+    for c in fetch:
+        c.start()
 
     across = [
         copy(cot_in.at[piece(i)], cot.at[2, piece(i)], cot_ss.at[0, i], cot_rs.at[0, i], at(dxl=1))
@@ -76,15 +100,18 @@
         for r in (4, 3, 5, 2, 6, 1, 7)
     }
     along_y = {
-        k: copy(kv.at[0], kv.at[k], y_ss.at[k], y_rs.at[k], at(dy=-YSTEP[k])) for k in (1, 2, 3)
+        (k, p): copy(kv.at[0, half_at(p)], kv.at[k, half_at(p)], y_ss.at[k, p], y_rs.at[k, p], at(dy=-YSTEP[k]))
+        for k in (1, 2, 3) for p in (NEAR, FAR)
     }
     swap_q = copy(q_in, qa.at[1], x_ss.at[0], x_rs.at[0], at(dxh=1))
     swap_l = copy(lse_in, lse2.at[1], x_ss.at[1], x_rs.at[1], at(dxh=1))
     swap_d = copy(delta2.at[0], delta2.at[1], x_ss.at[2], x_rs.at[2], at(dxh=1))
     swap_a = copy(da.at[0], da.at[1], x_ss.at[3], x_rs.at[3], at(dxh=1))
     back_y = {
-        k: copy(psend.at[k - 1], precv.at[k - 1], r_ss.at[k], r_rs.at[k], at(dy=YSTEP[k]))
-        for k in (1, 2, 3)
+        (k, p): copy(
+            psend.at[k - 1, half_at(p)], precv.at[k - 1, half_at(p)], r_ss.at[k, p], r_rs.at[k, p], at(dy=YSTEP[k])
+        )
+        for k in (1, 2, 3) for p in (FAR, NEAR)
     }
     back_z = {
         r: copy(zsend.at[PLACE[r]], zrecv.at[r - 1], g_ss.at[r], g_rs.at[r], at(dz=r))
@@ -92,16 +119,17 @@
     }
     back_q = copy(dqs, dqr, dq_ss.at[0], dq_rs.at[0], at(dxh=1))
 
+    pl.semaphore_wait(barrier, len(partners))
     for c in across:
         c.start()
+    fetch[0].wait()
+    fetch[1].wait()
+    for p in (NEAR, FAR):
+        for r in HALF_R[p]:
+            along_z[NZD - r].start()
     beside.start()
-    kv[0, PLACE[0], 0] = k_in[...]
-    kv[0, PLACE[0], 1] = v_in[...]
-    for c in along_z.values():
-        c.start()
-
-    qa[0] = q_in[...]
-    lse2[0] = lse_in[...]
+    fetch[2].wait()
+    fetch[4].wait()
     qx[...] = jnp.zeros_like(qx)
     dx[...] = jnp.zeros_like(dx)
     dq_t[...] = jnp.zeros_like(dq_t)
@@ -121,28 +149,40 @@
             dx[half, h, WIDTH : WIDTH + 16, :] = aug_rows(delta2[half, h : h + 1, :])
 
     widen_q(0)
-    attn_t = attn_in[...].T
-
-    for i in range(PIECES):
+    fetch[3].wait()
+    attn_t = attn[...].T
+
+    def pass_on(i):
         across[i].wait_recv()
         onward[i].start()
+
+    def spread(p):
+        for r in HALF_R[p]:
+            along_z[NZD - r].wait_recv()
+        for k in (1, 2):
+            along_y[k, p].start()
+
+    pass_on(0)
+    spread(NEAR)
+    pass_on(1)
+    pass_on(2)
+    pass_on(3)
+    spread(FAR)
     swap_q.start()
     swap_l.start()
-    for c in along_z.values():
-        c.wait_recv()
-    for k in (1, 2, 3):
-        along_y[k].start()
+    fetch[5].wait()
+    fetch[6].wait()
     beside.wait_recv()
 
     def block(dxl, dc):
         which = ((xl + dxl) % 2) * 2 + (core + dc) % 2
-        return w_in[:, pl.ds(pl.multiple_of(which * WIDTH, WIDTH), WIDTH)]
+        return w[:, pl.ds(pl.multiple_of(which * WIDTH, WIDTH), WIDTH)]
 
     weight = jnp.concatenate([block(0, 0), block(0, 1), block(1, 0), block(1, 1)], 1)
     for i in range(PIECES):
         onward[i].wait_recv()
         rows = pl.ds(i * PROWS, PROWS)
-        wide = jnp.concatenate([cot_in[rows, :], cot[1, rows], cot[2, rows], cot[3, rows]], 1)
+        wide = jnp.concatenate([cot[0, rows], cot[1, rows], cot[2, rows], cot[3, rows]], 1)
         da[0, rows] = lax.dot_general(
             wide, weight, (((1,), (1,)), ((), ())), preferred_element_type=F32
         ).astype(BF)
@@ -160,17 +200,23 @@
     tile = 256
 
     def step(u, _):
-        half, m = u // 8, u % 8
-        k = half * 3 + (1 - 2 * half) * (m // 2)
-        first = (m % 2) * 4
-
-        for cls in (1, 2, 3):
-
-            @pl.when(u == 2 * cls)
+        def pick(column):
+            return sum(jnp.where(u == i, unit[column], 0) for i, unit in enumerate(UNITS) if unit[column])
+
+        half, k, first = pick(0), pick(1), pick(2) * 4
+
+        @pl.when(u == 1)
+        def _():
+            along_y[3, NEAR].start()
+            along_y[3, FAR].start()
+
+        for cls, p in along_y:
+
+            @pl.when(u == TURN[0, cls, p])
             def _():
-                along_y[cls].wait_recv()
-
-        @pl.when(u == 8)
+                along_y[cls, p].wait_recv()
+
+        @pl.when(u == UNITS.index((1, 3, FAR)))
         def _():
             swap_q.wait_recv()
             swap_l.wait_recv()
@@ -202,32 +248,40 @@
         acc[k, places, 0] += grad_k.reshape(4, SHARD, WIDTH)
         acc[k, places, 1] += grad_v.reshape(4, SHARD, WIDTH)
 
-        for cls in (3, 2, 1):
-
-            @pl.when(u == 15 - 2 * cls)
+        for cls, p in back_y:
+
+            @pl.when(u == TURN[1, cls, p])
             def _():
-                psend[cls - 1] = acc[cls].astype(BF)
-                back_y[cls].start()
+                psend[cls - 1, half_at(p)] = acc[cls, half_at(p)].astype(BF)
+                back_y[cls, p].start()
+
+        @pl.when(u == TURN[1, 0, NEAR])
+        def _():
+            dqs[...] = (dq_t[1].T * 0.125).astype(BF)
+            back_q.start()
+            gather(FAR)
 
         return 0
 
-    lax.fori_loop(0, 16, step, 0)
-
-    dqs[...] = (dq_t[1].T * 0.125).astype(BF)
-    back_q.start()
-    for cls in (3, 2, 1):
-        back_y[cls].wait_recv()
-    line = acc[0]
-    for cls in (3, 2, 1):
-        line = line + precv[cls - 1].astype(F32)
-    acc[0] = line
-    zsend[...] = line.astype(BF)
-    for c in back_z.values():
-        c.start()
-    mine = (dq_t[0].T * 0.125).astype(F32)
+    def gather(p):
+        half = half_at(p)
+        for cls in (3, 1, 2):
+            back_y[cls, p].wait_recv()
+        line = acc[0, half]
+        for cls in (3, 1, 2):
+            line = line + precv[cls - 1, half].astype(F32)
+        acc[0, half] = line
+        zsend[half] = line.astype(BF)
+        for r in HALF_R[p]:
+            back_z[r].start()
+
+    lax.fori_loop(0, len(UNITS), step, 0)
+
+    gather(NEAR)
+    mine = dq_t[0].T * 0.125
     total = acc[0, PLACE[0]]
-    for r, c in back_z.items():
-        c.wait_recv()
+    for r in HALF_R[FAR] + HALF_R[NEAR]:
+        back_z[r].wait_recv()
         total = total + zrecv[r - 1].astype(F32)
     dk_out[...] = total[0].astype(BF)
     dv_out[...] = total[1].astype(BF)
@@ -251,9 +305,12 @@
             jax.ShapeDtypeStruct((SHARD, WIDTH), BF),
             jax.ShapeDtypeStruct((SHARD, WIDTH), BF),
         ],
-        in_specs=[vmem] * 7,
+        in_specs=[pl.BlockSpec(memory_space=pl.ANY)] * 7,
         out_specs=[vmem] * 3,
         scratch_shapes=[
+            pltpu.VMEM((ROWS, WIDTH), BF),
+            pltpu.VMEM((WIDTH, 4 * WIDTH), BF),
+            dma((7,)),
             pltpu.VMEM((4, ROWS, WIDTH), BF),
             pltpu.VMEM((2, ROWS, WIDTH), BF),
             pltpu.VMEM((2, ROWS, WIDTH), BF),
@@ -274,14 +331,14 @@
             pltpu.VMEM((ROWS, WIDTH), BF),
             dma((3, PIECES)), dma((3, PIECES)),
             dma((NZD,)), dma((NZD,)),
+            dma((4, 2)), dma((4, 2)),
             dma((4,)), dma((4,)),
-            dma((4,)), dma((4,)),
-            dma((4,)), dma((4,)),
+            dma((4, 2)), dma((4, 2)),
             dma((NZD,)), dma((NZD,)),
             dma((1,)), dma((1,)),
         ],
         compiler_params=pltpu.CompilerParams(
-            has_side_effects=True, vmem_limit_bytes=48 * 2**20
+            collective_id=0, has_side_effects=True, vmem_limit_bytes=56 * 2**20
         ),
         cost_estimate=pl.CostEstimate(
             flops=11 * 10**9, bytes_accessed=3 * 2**20, transcendentals=2**23

time: 75.1 us -> 56.8 us (0.76)
  the two profiles are of different devices: /device:TPU:2 before, /device:TPU:1 now
where the time goes in v2:
time: 56.8 us; the launch traced here: 56.7 us
  Pallas kernels  53 us (93%)
  local copies, waits for them, and re-layouts  3.01 us (5%)
  between operations  0.65 us (1%)
    pallas_call x1, Pallas kernels, body(): pl.pallas_call(kernel, out_shape=[jax.ShapeDtypeStruct((ROWS, WIDTH), BF)...  53 us
    unnamed x7, local copies, waits for them, and re-layouts  3.01 us

profile of v2, /device:TPU:1, one launch (start us, length us, event | category | flops | bytes accessed | tf_op | source)
XLA Modules:
  0.0 56.7 jit_solution(8131872410653686168)
XLA Ops:
  0.6 53.0 %shard_map.94 = (bf16[1024,128]{1,0:T(8,128)(2,1)}, bf16[64,128]{1,0:T(8,128)(2,1)}, bf16[64,128]{1,0:T(8,128)(2,1)}) custom-call(bf16[1024,128]{1,0:T(8,128)(2,1)} %q_in.1, bf16[64,128]{1,0:T(8,128)(2,1)} %k_in.1, bf16[64,128]{1,0:T(8,128)(2,1)} %v_in.1, bf16[1024,128]{1,0:T(8,128)(2,1)} %attn_in.1, bf16[1024,128]{1,0:T(8,128)(2,1)} %cot_in.1, ...), custom_call_target="tpu_custom_call" | custom-call | flops 11000000512 | bytes 3145728 | tf_op jit(solution)/shard_map/pallas_call | solution.py:301
  53.7 0.0 copy-start.1
  53.7 1.7 %copy.13 = bf16[1024,128]{1,0:T(8,128)(2,1)} copy(bf16[1024,128]{1,0:T(8,128)(2,1)} %get-tuple-element.6) | data formatting | bytes 524288
  55.4 0.0 copy-done.1
  55.4 0.0 copy-start
  55.4 0.6 %copy.14 = bf16[64,128]{1,0:T(8,128)(2,1)} copy(bf16[64,128]{1,0:T(8,128)(2,1)S(1)} %copy-done.1) | data formatting | bytes 32768
  56.0 0.1 copy-done
  56.1 0.6 %copy.15 = bf16[64,128]{1,0:T(8,128)(2,1)} copy(bf16[64,128]{1,0:T(8,128)(2,1)S(1)} %copy-done) | data formatting | bytes 32768
Async XLA Ops:
  53.7 1.7 %copy-start.1 = (bf16[64,128]{1,0:T(8,128)(2,1)S(1)}, bf16[64,128]{1,0:T(8,128)(2,1)}, u32[]{:S(2)}) copy-start(bf16[64,128]{1,0:T(8,128)(2,1)} %get-tuple-element.7) | copy-start | bytes 49156
  55.4 0.7 %copy-start = (bf16[64,128]{1,0:T(8,128)(2,1)S(1)}, bf16[64,128]{1,0:T(8,128)(2,1)}, u32[]{:S(2)}) copy-start(bf16[64,128]{1,0:T(8,128)(2,1)} %get-tuple-element.8) | copy-start | bytes 49156

commit v3 on v2

--- a/solution.py
+++ b/solution.py
@@ -25,6 +25,8 @@
     (1, 3, FAR), (1, 1, FAR), (1, 2, FAR), (1, 0, FAR), (1, 3, NEAR), (1, 1, NEAR), (1, 2, NEAR), (1, 0, NEAR),
     (0, 0, NEAR),
 )
+TILE = 256
+FIRST_SWAPPED = [half for half, _, _ in UNITS].index(1)
 TURN = {unit: i for i, unit in enumerate(UNITS)}
 HALF_R = {FAR: (4, 3, 5, 2), NEAR: (6, 1, 7)}
 PIECES = 4
@@ -35,20 +37,29 @@
     return jnp.dot(a, b, preferred_element_type=F32)
 
 
+def nt(a, b):
+    return lax.dot_general(a, b, (((1,), (1,)), ((), ())), preferred_element_type=F32)
+
+
 def three(row):
     a = row.astype(BF).astype(F32)
     b = (row - a).astype(BF).astype(F32)
     return [a, b, row - a - b]
 
 
-def aug_rows(row):
-    return jnp.concatenate([*three(row), jnp.zeros((13, row.shape[1]), F32)], 0).astype(BF)
+def columns(rows):
+    n = rows.shape[1]
+    pad = jnp.zeros((5, n), F32)
+    parts = [p for h in range(2) for p in (*three(rows[h : h + 1, :]), pad)]
+    low = jnp.concatenate(parts, 0).astype(BF)
+    return jnp.concatenate([low, jnp.zeros((WIDTH - 16, n), BF)], 0).T
 
 
 def kernel(
     q_in, k_in, v_in, attn_in, cot_in, w_in, lse_in,
     dq_out, dk_out, dv_out,
-    attn, w, in_sem, cot, qa, da, lse2, delta2, qx, dx, kv, acc, psend, precv, zsend, zrecv, p_t, s_t, dq_t, dqs, dqr,
+    attn, w, in_sem, cot, qa, da, lse2, delta2, qx, dx, q_t, d_t, kv, acc, psend, precv, zsend, zrecv, owned,
+    probs, grads, dq, dqs, dqr,
     cot_ss, cot_rs, z_ss, z_rs, y_ss, y_rs, x_ss, x_rs, r_ss, r_rs, g_ss, g_rs, dq_ss, dq_rs,
 ):
     link, head = lax.axis_index("links"), lax.axis_index("heads")
@@ -109,7 +120,7 @@
     swap_a = copy(da.at[0], da.at[1], x_ss.at[3], x_rs.at[3], at(dxh=1))
     back_y = {
         (k, p): copy(
-            psend.at[k - 1, half_at(p)], precv.at[k - 1, half_at(p)], r_ss.at[k, p], r_rs.at[k, p], at(dy=YSTEP[k])
+            psend.at[k - 1, p], precv.at[k - 1, p], r_ss.at[k, p], r_rs.at[k, p], at(dy=YSTEP[k])
         )
         for k in (1, 2, 3) for p in (FAR, NEAR)
     }
@@ -130,23 +141,30 @@
     beside.start()
     fetch[2].wait()
     fetch[4].wait()
-    qx[...] = jnp.zeros_like(qx)
-    dx[...] = jnp.zeros_like(dx)
-    dq_t[...] = jnp.zeros_like(dq_t)
+    dq[...] = jnp.zeros_like(dq)
     acc[...] = jnp.zeros_like(acc)
 
+    lane = lax.broadcasted_iota(jnp.int32, (1, WIDTH), 1)
+
+    def one_head(h):
+        return jnp.where(lane // DH == h, 1.0, 0.0)
+
+    def one_group(h):
+        return jnp.where(lane // 8 == h, 1.0, 0.0).astype(BF)
+
     def widen_q(half):
-        turned = qa[half].T
+        tokens = qa[half]
+        q_t[half] = (tokens * jnp.full((1, WIDTH), 0.125, BF)).T
+        extra = columns(lse2[half])
         for h in range(2):
-            own = slice(DH * h, DH * h + DH)
-            qx[half, h, own, :] = (turned[own].astype(F32) * 0.125).astype(BF)
-            qx[half, h, WIDTH : WIDTH + 16, :] = aug_rows(lse2[half, h : h + 1, :])
-
-    def widen_d(half, turned):
+            qx[half, h, :, :WIDTH] = tokens * (one_head(h) * 0.125).astype(BF)
+            qx[half, h, :, WIDTH:] = extra * one_group(h)
+
+    def widen_d(half, rows, tokens):
+        extra = columns(delta2[half, :, rows])
         for h in range(2):
-            own = slice(DH * h, DH * h + DH)
-            dx[half, h, own, :] = turned[own]
-            dx[half, h, WIDTH : WIDTH + 16, :] = aug_rows(delta2[half, h : h + 1, :])
+            dx[half, h, rows, :WIDTH] = tokens * one_head(h).astype(BF)
+            dx[half, h, rows, WIDTH:] = extra * one_group(h)
 
     widen_q(0)
     fetch[3].wait()
@@ -179,114 +197,138 @@
         return w[:, pl.ds(pl.multiple_of(which * WIDTH, WIDTH), WIDTH)]
 
     weight = jnp.concatenate([block(0, 0), block(0, 1), block(1, 0), block(1, 1)], 1)
+    row = lax.broadcasted_iota(jnp.int32, (WIDTH, CHUNK), 0)
+    minus = jnp.where(row < 16, -1.0, 0.0).astype(BF)
+    left = lax.broadcasted_iota(jnp.int32, (TILE, WIDTH), 1) < DH
+    tiles = range(ROWS // TILE)
+
+    def unit(half, k, p):
+        places = pl.ds(p * 4, 4)
+        keys = kv[k, places, 0].reshape(CHUNK, WIDTH)
+        values = kv[k, places, 1].reshape(CHUNK, WIDTH)
+        right_k = jnp.concatenate([keys.T, minus], 0)
+        right_v = jnp.concatenate([values.T, minus], 0)
+
+        def tile(h, j):
+            rows = slice(j * TILE, (j + 1) * TILE)
+            scores = mm(qx[half, h, rows, :], right_k)
+            moved = mm(dx[half, h, rows, :], right_v)
+            prob = jnp.exp2(scores * LOG2E)
+            probs[h, rows, :] = prob.astype(BF)
+            grads[h, rows, :] = (prob * moved).astype(BF)
+
+        def zones(h):
+            own = slice(DH * h, DH * h + DH)
+            acc[k, p, 0, own, :] += mm(q_t[half, own, :], grads[h])
+            acc[k, p, 1, own, :] += mm(d_t[half, own, :], probs[h])
+
+        def links(j):
+            rows = slice(j * TILE, (j + 1) * TILE)
+            dq[half, rows, :] += jnp.where(left, mm(grads[0, rows, :], keys), mm(grads[1, rows, :], keys))
+
+        return tile, zones, links
+
+    tile, zones, links = unit(*UNITS[0])
     for i in range(PIECES):
         onward[i].wait_recv()
         rows = pl.ds(i * PROWS, PROWS)
         wide = jnp.concatenate([cot[0, rows], cot[1, rows], cot[2, rows], cot[3, rows]], 1)
-        da[0, rows] = lax.dot_general(
-            wide, weight, (((1,), (1,)), ((), ())), preferred_element_type=F32
-        ).astype(BF)
+        tokens = nt(wide, weight).astype(BF)
+        da[0, rows] = tokens
+        turned = tokens.T
+        d_t[0, :, rows] = turned
+        product = turned.astype(F32) * attn_t[:, i * PROWS : (i + 1) * PROWS].astype(F32)
+        for h in range(2):
+            delta2[0, h : h + 1, rows] = jnp.sum(product[DH * h : DH * h + DH], axis=0, keepdims=True)
+        widen_d(0, rows, tokens)
+        for h in range(2):
+            tile(h, i)
     swap_a.start()
-    turned = da[0].T
-    product = turned.astype(F32) * attn_t.astype(F32)
+    swap_d.start()
     for h in range(2):
-        delta2[0, h : h + 1, :] = jnp.sum(product[DH * h : DH * h + DH], axis=0, keepdims=True)
-    swap_d.start()
-    widen_d(0, turned)
-
-    lane = lax.broadcasted_iota(jnp.int32, (CHUNK, WIDTH), 1)
-    minus = jnp.where(lane < 3, -1.0, 0.0).astype(BF)
-    left = lane < DH
-    tile = 256
+        zones(h)
+    for j in tiles:
+        links(j)
 
     def step(u, _):
         def pick(column):
             return sum(jnp.where(u == i, unit[column], 0) for i, unit in enumerate(UNITS) if unit[column])
 
-        half, k, first = pick(0), pick(1), pick(2) * 4
+        half, k, p = pick(0), pick(1), pick(2)
 
         @pl.when(u == 1)
         def _():
             along_y[3, NEAR].start()
             along_y[3, FAR].start()
 
-        for cls, p in along_y:
-
-            @pl.when(u == TURN[0, cls, p])
+        for cls, part in along_y:
+
+            @pl.when(u == TURN[0, cls, part])
             def _():
-                along_y[cls, p].wait_recv()
-
-        @pl.when(u == UNITS.index((1, 3, FAR)))
+                along_y[cls, part].wait_recv()
+
+        @pl.when(u == FIRST_SWAPPED)
         def _():
             swap_q.wait_recv()
             swap_l.wait_recv()
             swap_d.wait_recv()
             swap_a.wait_recv()
             widen_q(1)
-            widen_d(1, da[1].T)
-
-        places = pl.ds(first, 4)
-        keys = kv[k, places, 0].reshape(CHUNK, WIDTH)
-        values = kv[k, places, 1].reshape(CHUNK, WIDTH)
-        wide_k = jnp.concatenate([keys, minus], 1)
-        wide_v = jnp.concatenate([values, minus], 1)
-        keys_t = keys.T
-        outs = []
-        for h in range(2):
-            for j in range(ROWS // tile):
-                cols = slice(j * tile, (j + 1) * tile)
-                scores = mm(wide_k, qx[half, h, :, cols])
-                moved = mm(wide_v, dx[half, h, :, cols])
-                probs = jnp.exp2(scores * LOG2E)
-                p_t[h, :, cols] = probs.astype(BF)
-                s_t[h, :, cols] = (probs * moved).astype(BF)
-            own = slice(DH * h, DH * h + DH)
-            outs.append((mm(s_t[h], qa[half]), mm(p_t[h], da[half])))
-            dq_t[half, own, :] += mm(keys_t[own], s_t[h])
-        grad_k = jnp.where(left, outs[0][0], outs[1][0]) * 0.125
-        grad_v = jnp.where(left, outs[0][1], outs[1][1])
-        acc[k, places, 0] += grad_k.reshape(4, SHARD, WIDTH)
-        acc[k, places, 1] += grad_v.reshape(4, SHARD, WIDTH)
+            tokens = da[1]
+            d_t[1] = tokens.T
+            widen_d(1, pl.ds(0, ROWS), tokens)
+
+        tile, zones, links = unit(half, k, p)
+        for j in tiles:
+            tile(0, j)
+        tile(1, 0)
+        zones(0)
+        for j in tiles[1:]:
+            tile(1, j)
+        zones(1)
+        for j in tiles:
+            links(j)
 
         for cls, p in back_y:
 
             @pl.when(u == TURN[1, cls, p])
             def _():
-                psend[cls - 1, half_at(p)] = acc[cls, half_at(p)].astype(BF)
+                psend[cls - 1, p] = acc[cls, p].astype(BF)
                 back_y[cls, p].start()
 
         @pl.when(u == TURN[1, 0, NEAR])
         def _():
-            dqs[...] = (dq_t[1].T * 0.125).astype(BF)
+            dqs[...] = (dq[1] * 0.125).astype(BF)
             back_q.start()
             gather(FAR)
 
         return 0
 
     def gather(p):
-        half = half_at(p)
         for cls in (3, 1, 2):
             back_y[cls, p].wait_recv()
-        line = acc[0, half]
-        for cls in (3, 1, 2):
-            line = line + precv[cls - 1, half].astype(F32)
-        acc[0, half] = line
-        zsend[half] = line.astype(BF)
+        for t in range(2):
+            line = acc[0, p, t]
+            for cls in (3, 1, 2):
+                line = line + precv[cls - 1, p, t].astype(F32)
+            shards = line.T.reshape(4, SHARD, WIDTH)
+            zsend[half_at(p), t] = shards.astype(BF)
+            if p == NEAR:
+                owned[t] = shards[PLACE[0] - 4]
         for r in HALF_R[p]:
             back_z[r].start()
 
-    lax.fori_loop(0, len(UNITS), step, 0)
+    lax.fori_loop(1, len(UNITS), step, 0)
 
     gather(NEAR)
-    mine = dq_t[0].T * 0.125
-    total = acc[0, PLACE[0]]
+    total = owned[...]
     for r in HALF_R[FAR] + HALF_R[NEAR]:
         back_z[r].wait_recv()
         total = total + zrecv[r - 1].astype(F32)
     dk_out[...] = total[0].astype(BF)
     dv_out[...] = total[1].astype(BF)
     back_q.wait_recv()
-    dq_out[...] = (mine + dqr[...].astype(F32)).astype(BF)
+    dq_out[...] = (dq[0] * 0.125 + dqr[...].astype(F32)).astype(BF)
 
     for c in (
         *across, beside, *onward, *along_z.values(), *along_y.values(), swap_q, swap_l, swap_d, swap_a,
@@ -316,17 +358,20 @@
             pltpu.VMEM((2, ROWS, WIDTH), BF),
             pltpu.VMEM((2, 2, ROWS), F32),
             pltpu.VMEM((2, 2, ROWS), F32),
-            pltpu.VMEM((2, 2, AUG, ROWS), BF),
-            pltpu.VMEM((2, 2, AUG, ROWS), BF),
+            pltpu.VMEM((2, 2, ROWS, AUG), BF),
+            pltpu.VMEM((2, 2, ROWS, AUG), BF),
+            pltpu.VMEM((2, WIDTH, ROWS), BF),
+            pltpu.VMEM((2, WIDTH, ROWS), BF),
             pltpu.VMEM((4, NZD, 2, SHARD, WIDTH), BF),
-            pltpu.VMEM((4, NZD, 2, SHARD, WIDTH), F32),
-            pltpu.VMEM((3, NZD, 2, SHARD, WIDTH), BF),
-            pltpu.VMEM((3, NZD, 2, SHARD, WIDTH), BF),
+            pltpu.VMEM((4, 2, 2, WIDTH, CHUNK), F32),
+            pltpu.VMEM((3, 2, 2, WIDTH, CHUNK), BF),
+            pltpu.VMEM((3, 2, 2, WIDTH, CHUNK), BF),
             pltpu.VMEM((NZD, 2, SHARD, WIDTH), BF),
             pltpu.VMEM((NZD - 1, 2, SHARD, WIDTH), BF),
-            pltpu.VMEM((2, CHUNK, ROWS), BF),
-            pltpu.VMEM((2, CHUNK, ROWS), BF),
-            pltpu.VMEM((2, WIDTH, ROWS), F32),
+            pltpu.VMEM((2, SHARD, WIDTH), F32),
+            pltpu.VMEM((2, ROWS, CHUNK), BF),
+            pltpu.VMEM((2, ROWS, CHUNK), BF),
+            pltpu.VMEM((2, ROWS, WIDTH), F32),
             pltpu.VMEM((ROWS, WIDTH), BF),
             pltpu.VMEM((ROWS, WIDTH), BF),
             dma((3, PIECES)), dma((3, PIECES)),

time: 56.8 us -> 54.2 us (0.954)
  the two profiles are of different devices: /device:TPU:1 before, /device:TPU:8 now
where the time goes in v3:
time: 54.2 us; the launch traced here: 54 us
  Pallas kernels  50.4 us (93%)
  local copies, waits for them, and re-layouts  3.01 us (6%)
  between operations  0.65 us (1%)
    pallas_call x1, Pallas kernels, body(): pl.pallas_call(kernel, out_shape=[jax.ShapeDtypeStruct((ROWS, WIDTH), BF)...  50.4 us
    unnamed x7, local copies, waits for them, and re-layouts  3.01 us

profile of v3, /device:TPU:8, one launch (start us, length us, event | category | flops | bytes accessed | tf_op | source)
XLA Modules:
  0.0 54.0 jit_solution(1663794388238173860)
XLA Ops:
  0.6 50.4 %shard_map.94 = (bf16[1024,128]{1,0:T(8,128)(2,1)}, bf16[64,128]{1,0:T(8,128)(2,1)}, bf16[64,128]{1,0:T(8,128)(2,1)}) custom-call(bf16[1024,128]{1,0:T(8,128)(2,1)} %q_in.1, bf16[64,128]{1,0:T(8,128)(2,1)} %k_in.1, bf16[64,128]{1,0:T(8,128)(2,1)} %v_in.1, bf16[1024,128]{1,0:T(8,128)(2,1)} %attn_in.1, bf16[1024,128]{1,0:T(8,128)(2,1)} %cot_in.1, ...), custom_call_target="tpu_custom_call" | custom-call | flops 11000000512 | bytes 3145728 | tf_op jit(solution)/shard_map/pallas_call | solution.py:343
  51.0 0.0 copy-start.1
  51.0 1.7 %copy.13 = bf16[1024,128]{1,0:T(8,128)(2,1)} copy(bf16[1024,128]{1,0:T(8,128)(2,1)} %get-tuple-element.6) | data formatting | bytes 524288
  52.7 0.0 copy-done.1
  52.7 0.0 copy-start
  52.7 0.6 %copy.14 = bf16[64,128]{1,0:T(8,128)(2,1)} copy(bf16[64,128]{1,0:T(8,128)(2,1)S(1)} %copy-done.1) | data formatting | bytes 32768
  53.3 0.1 copy-done
  53.4 0.6 %copy.15 = bf16[64,128]{1,0:T(8,128)(2,1)} copy(bf16[64,128]{1,0:T(8,128)(2,1)S(1)} %copy-done) | data formatting | bytes 32768
Async XLA Ops:
  51.0 1.7 %copy-start.1 = (bf16[64,128]{1,0:T(8,128)(2,1)S(1)}, bf16[64,128]{1,0:T(8,128)(2,1)}, u32[]{:S(2)}) copy-start(bf16[64,128]{1,0:T(8,128)(2,1)} %get-tuple-element.7) | copy-start | bytes 49156
  52.7 0.7 %copy-start = (bf16[64,128]{1,0:T(8,128)(2,1)S(1)}, bf16[64,128]{1,0:T(8,128)(2,1)}, u32[]{:S(2)}) copy-start(bf16[64,128]{1,0:T(8,128)(2,1)} %get-tuple-element.8) | copy-start | bytes 49156

commit v4 on v3

--- a/solution.py
+++ b/solution.py
@@ -18,16 +18,8 @@
 AUG = 256
 ORDER = (4, 3, 5, 2, 6, 1, 7, 0)
 PLACE = {r: i for i, r in enumerate(ORDER)}
-YSTEP = (0, 1, 3, 2)
 FAR, NEAR = 0, 1
-UNITS = (
-    (0, 0, FAR), (0, 1, NEAR), (0, 2, NEAR), (0, 1, FAR), (0, 2, FAR), (0, 3, NEAR), (0, 3, FAR),
-    (1, 3, FAR), (1, 1, FAR), (1, 2, FAR), (1, 0, FAR), (1, 3, NEAR), (1, 1, NEAR), (1, 2, NEAR), (1, 0, NEAR),
-    (0, 0, NEAR),
-)
 TILE = 256
-FIRST_SWAPPED = [half for half, _, _ in UNITS].index(1)
-TURN = {unit: i for i, unit in enumerate(UNITS)}
 HALF_R = {FAR: (4, 3, 5, 2), NEAR: (6, 1, 7)}
 PIECES = 4
 PROWS = ROWS // PIECES
@@ -57,10 +49,10 @@
 
 def kernel(
     q_in, k_in, v_in, attn_in, cot_in, w_in, lse_in,
-    dq_out, dk_out, dv_out,
+    mine_out, dqr, dk_out, dv_out,
     attn, w, in_sem, cot, qa, da, lse2, delta2, qx, dx, q_t, d_t, kv, acc, psend, precv, zsend, zrecv, owned,
-    probs, grads, dq, dqs, dqr,
-    cot_ss, cot_rs, z_ss, z_rs, y_ss, y_rs, x_ss, x_rs, r_ss, r_rs, g_ss, g_rs, dq_ss, dq_rs,
+    probs, grads, dq, dqs, zsend2, zrecv2, owned2, send2, recv2,
+    cot_ss, cot_rs, z_ss, z_rs, y_ss, y_rs, x_ss, x_rs, r_ss, r_rs, g_ss, g_rs, dq_ss, dq_rs, t_ss, t_rs, out_sem,
 ):
     link, head = lax.axis_index("links"), lax.axis_index("heads")
     xh, z, y = link // (NZD * NYD), (link // NYD) % NZD, link % NYD
@@ -110,25 +102,33 @@
         r: copy(shard, kv.at[0, PLACE[(NZD - r) % NZD]], z_ss.at[r], z_rs.at[r], at(dz=r))
         for r in (4, 3, 5, 2, 6, 1, 7)
     }
-    along_y = {
-        (k, p): copy(kv.at[0, half_at(p)], kv.at[k, half_at(p)], y_ss.at[k, p], y_rs.at[k, p], at(dy=-YSTEP[k]))
-        for k in (1, 2, 3) for p in (NEAR, FAR)
-    }
+    def along_y(k, p):
+        part = half_at(p)
+        return copy(kv.at[0, part], kv.at[k, part], y_ss.at[k, p], y_rs.at[k, p], at(dy=-k))
+
     swap_q = copy(q_in, qa.at[1], x_ss.at[0], x_rs.at[0], at(dxh=1))
     swap_l = copy(lse_in, lse2.at[1], x_ss.at[1], x_rs.at[1], at(dxh=1))
     swap_d = copy(delta2.at[0], delta2.at[1], x_ss.at[2], x_rs.at[2], at(dxh=1))
-    swap_a = copy(da.at[0], da.at[1], x_ss.at[3], x_rs.at[3], at(dxh=1))
-    back_y = {
-        (k, p): copy(
-            psend.at[k - 1, p], precv.at[k - 1, p], r_ss.at[k, p], r_rs.at[k, p], at(dy=YSTEP[k])
-        )
-        for k in (1, 2, 3) for p in (FAR, NEAR)
-    }
+    swap_a = [
+        copy(da.at[0, piece(i)], da.at[1, piece(i)], x_ss.at[3 + i], x_rs.at[3 + i], at(dxh=1))
+        for i in range(PIECES)
+    ]
+    def back_y(k, p):
+        return copy(psend.at[k - 1, p], precv.at[k - 1, p], r_ss.at[k, p], r_rs.at[k, p], at(dy=k))
+
     back_z = {
         r: copy(zsend.at[PLACE[r]], zrecv.at[r - 1], g_ss.at[r], g_rs.at[r], at(dz=r))
         for r in (4, 3, 5, 2, 6, 1, 7)
     }
-    back_q = copy(dqs, dqr, dq_ss.at[0], dq_rs.at[0], at(dxh=1))
+    back_z2 = {
+        r: copy(zsend2.at[PLACE[r]], zrecv2.at[r - 1], t_ss.at[r], t_rs.at[r], at(dz=r))
+        for r in (4, 3, 5, 2, 6, 1, 7)
+    }
+    across_y = copy(send2, recv2, t_ss.at[0], t_rs.at[0], at(dy=2))
+    back_q = [
+        copy(dqs.at[part], dqr.at[part], dq_ss.at[i], dq_rs.at[i], at(dxh=1))
+        for i, part in enumerate((pl.ds(0, ROWS // 2), pl.ds(ROWS // 2, ROWS // 2)))
+    ]
 
     pl.semaphore_wait(barrier, len(partners))
     for c in across:
@@ -177,17 +177,17 @@
     def spread(p):
         for r in HALF_R[p]:
             along_z[NZD - r].wait_recv()
-        for k in (1, 2):
-            along_y[k, p].start()
+        for k in (1, 3):
+            along_y(k, p).start()
 
     pass_on(0)
     spread(NEAR)
     pass_on(1)
     pass_on(2)
+    swap_q.start()
+    swap_l.start()
     pass_on(3)
     spread(FAR)
-    swap_q.start()
-    swap_l.start()
     fetch[5].wait()
     fetch[6].wait()
     beside.wait_recv()
@@ -219,8 +219,10 @@
 
         def zones(h):
             own = slice(DH * h, DH * h + DH)
-            acc[k, p, 0, own, :] += mm(q_t[half, own, :], grads[h])
-            acc[k, p, 1, own, :] += mm(d_t[half, own, :], probs[h])
+            grad_k = acc[k, p, 0, own, :] + mm(q_t[half, own, :], grads[h])
+            grad_v = acc[k, p, 1, own, :] + mm(d_t[half, own, :], probs[h])
+            acc[k, p, 0, own, :] = grad_k
+            acc[k, p, 1, own, :] = grad_v
 
         def links(j):
             rows = slice(j * TILE, (j + 1) * TILE)
@@ -228,13 +230,14 @@
 
         return tile, zones, links
 
-    tile, zones, links = unit(*UNITS[0])
+    tile, zones, links = unit(0, 0, FAR)
     for i in range(PIECES):
         onward[i].wait_recv()
         rows = pl.ds(i * PROWS, PROWS)
         wide = jnp.concatenate([cot[0, rows], cot[1, rows], cot[2, rows], cot[3, rows]], 1)
         tokens = nt(wide, weight).astype(BF)
         da[0, rows] = tokens
+        swap_a[i].start()
         turned = tokens.T
         d_t[0, :, rows] = turned
         product = turned.astype(F32) * attn_t[:, i * PROWS : (i + 1) * PROWS].astype(F32)
@@ -243,41 +246,15 @@
         widen_d(0, rows, tokens)
         for h in range(2):
             tile(h, i)
-    swap_a.start()
     swap_d.start()
+    along_y(2, NEAR).start()
+    along_y(2, FAR).start()
     for h in range(2):
         zones(h)
     for j in tiles:
         links(j)
 
-    def step(u, _):
-        def pick(column):
-            return sum(jnp.where(u == i, unit[column], 0) for i, unit in enumerate(UNITS) if unit[column])
-
-        half, k, p = pick(0), pick(1), pick(2)
-
-        @pl.when(u == 1)
-        def _():
-            along_y[3, NEAR].start()
-            along_y[3, FAR].start()
-
-        for cls, part in along_y:
-
-            @pl.when(u == TURN[0, cls, part])
-            def _():
-                along_y[cls, part].wait_recv()
-
-        @pl.when(u == FIRST_SWAPPED)
-        def _():
-            swap_q.wait_recv()
-            swap_l.wait_recv()
-            swap_d.wait_recv()
-            swap_a.wait_recv()
-            widen_q(1)
-            tokens = da[1]
-            d_t[1] = tokens.T
-            widen_d(1, pl.ds(0, ROWS), tokens)
-
+    def work(half, k, p):
         tile, zones, links = unit(half, k, p)
         for j in tiles:
             tile(0, j)
@@ -289,50 +266,107 @@
         for j in tiles:
             links(j)
 
-        for cls, p in back_y:
-
-            @pl.when(u == TURN[1, cls, p])
+    def own_step(i, _):
+        late = i // 4
+        k, p = (1 + 2 * (i % 2)) * (1 - late) + 2 * late, (1 - i // 2) * (1 - late) + (5 - i) * late
+        along_y(k, p).wait_recv()
+        work(0, k, p)
+        return 0
+
+    lax.fori_loop(0, 6, own_step, 0)
+
+    for c in (swap_q, swap_l, *swap_a, swap_d):
+        c.wait_recv()
+    widen_q(1)
+    for i in range(PIECES):
+        tokens = da[1, piece(i)]
+        d_t[1, :, piece(i)] = tokens.T
+        widen_d(1, piece(i), tokens)
+    def swapped_step(i, _):
+        k = jnp.where(i < 2, 2, jnp.where(i == 6, 0, 1 + 2 * (i % 2)))
+        p = jnp.where(i < 2, i, jnp.where(i == 6, 0, i // 4))
+        work(1, k, p)
+
+        for part in (FAR, NEAR):
+
+            @pl.when(i == part)
             def _():
+                turn(2, part, (), zsend2, owned2)
+                for r in HALF_R[part]:
+                    back_z2[r].start()
+
+        for first in (0, 1):
+
+            @pl.when((i == 2 + first) | (i == 4 + first))
+            def _():
+                cls = 1 + 2 * first
                 psend[cls - 1, p] = acc[cls, p].astype(BF)
-                back_y[cls, p].start()
-
-        @pl.when(u == TURN[1, 0, NEAR])
-        def _():
-            dqs[...] = (dq[1] * 0.125).astype(BF)
-            back_q.start()
-            gather(FAR)
+                back_y(cls, p).start()
 
         return 0
 
-    def gather(p):
-        for cls in (3, 1, 2):
-            back_y[cls, p].wait_recv()
+    def turn(k, p, others, target, keep):
         for t in range(2):
-            line = acc[0, p, t]
-            for cls in (3, 1, 2):
+            line = acc[k, p, t]
+            for cls in others:
                 line = line + precv[cls - 1, p, t].astype(F32)
             shards = line.T.reshape(4, SHARD, WIDTH)
-            zsend[half_at(p), t] = shards.astype(BF)
+            target[half_at(p), t] = shards.astype(BF)
             if p == NEAR:
-                owned[t] = shards[PLACE[0] - 4]
+                keep[t] = shards[PLACE[0] - 4]
+
+    def gather(p):
+        for cls in (1, 3):
+            back_y(cls, p).wait_recv()
+        turn(0, p, (1, 3), zsend, owned)
         for r in HALF_R[p]:
             back_z[r].start()
 
-    lax.fori_loop(1, len(UNITS), step, 0)
-
+    lax.fori_loop(0, 7, swapped_step, 0)
+
+    total = owned2[...]
+    for r in HALF_R[FAR] + HALF_R[NEAR]:
+        back_z2[r].wait_recv()
+        total = total + zrecv2[r - 1].astype(F32)
+    send2[...] = total.astype(BF)
+    across_y.start()
+    gather(FAR)
+
+    tile, zones, links = unit(1, 0, NEAR)
+    for i in range(2):
+        for j in tiles[2 * i : 2 * i + 2]:
+            for h in range(2):
+                tile(h, j)
+        for j in tiles[2 * i : 2 * i + 2]:
+            links(j)
+        rows = slice(i * (ROWS // 2), (i + 1) * (ROWS // 2))
+        dqs[rows, :] = (dq[1, rows, :] * 0.125).astype(BF)
+        back_q[i].start()
+    for h in range(2):
+        zones(h)
+
+    work(0, 0, NEAR)
+
+    out = pltpu.make_async_copy(dq.at[0], mine_out, out_sem)
+    out.start()
     gather(NEAR)
     total = owned[...]
+    across_y.wait_recv()
+    total = total + recv2[...].astype(F32)
     for r in HALF_R[FAR] + HALF_R[NEAR]:
         back_z[r].wait_recv()
         total = total + zrecv[r - 1].astype(F32)
     dk_out[...] = total[0].astype(BF)
     dv_out[...] = total[1].astype(BF)
-    back_q.wait_recv()
-    dq_out[...] = (dq[0] * 0.125 + dqr[...].astype(F32)).astype(BF)
+    for c in back_q:
+        c.wait_recv()
+    out.wait()
 
     for c in (
-        *across, beside, *onward, *along_z.values(), *along_y.values(), swap_q, swap_l, swap_d, swap_a,
-        *back_y.values(), *back_z.values(), back_q,
+        *across, beside, *onward, *along_z.values(), swap_q, swap_l, swap_d, *swap_a,
+        *back_z.values(), *back_z2.values(), across_y, *back_q,
+        *(along_y(k, p) for k in (1, 2, 3) for p in (FAR, NEAR)),
+        *(back_y(k, p) for k in (1, 3) for p in (FAR, NEAR)),
     ):
         c.wait_send()
 
@@ -340,15 +374,17 @@
 def body(queries, keys, values, attn, cotangent, out_weight, lse):
     vmem = pl.BlockSpec(memory_space=pltpu.VMEM)
     dma = pltpu.SemaphoreType.DMA
-    return pl.pallas_call(
+    anywhere = pl.BlockSpec(memory_space=pl.ANY)
+    mine, returned, key_grad, value_grad = pl.pallas_call(
         kernel,
         out_shape=[
+            jax.ShapeDtypeStruct((ROWS, WIDTH), F32),
             jax.ShapeDtypeStruct((ROWS, WIDTH), BF),
             jax.ShapeDtypeStruct((SHARD, WIDTH), BF),
             jax.ShapeDtypeStruct((SHARD, WIDTH), BF),
         ],
-        in_specs=[pl.BlockSpec(memory_space=pl.ANY)] * 7,
-        out_specs=[vmem] * 3,
+        in_specs=[anywhere] * 7,
+        out_specs=[anywhere, anywhere, vmem, vmem],
         scratch_shapes=[
             pltpu.VMEM((ROWS, WIDTH), BF),
             pltpu.VMEM((WIDTH, 4 * WIDTH), BF),
@@ -373,14 +409,20 @@
             pltpu.VMEM((2, ROWS, CHUNK), BF),
             pltpu.VMEM((2, ROWS, WIDTH), F32),
             pltpu.VMEM((ROWS, WIDTH), BF),
-            pltpu.VMEM((ROWS, WIDTH), BF),
+            pltpu.VMEM((NZD, 2, SHARD, WIDTH), BF),
+            pltpu.VMEM((NZD - 1, 2, SHARD, WIDTH), BF),
+            pltpu.VMEM((2, SHARD, WIDTH), F32),
+            pltpu.VMEM((2, SHARD, WIDTH), BF),
+            pltpu.VMEM((2, SHARD, WIDTH), BF),
             dma((3, PIECES)), dma((3, PIECES)),
             dma((NZD,)), dma((NZD,)),
             dma((4, 2)), dma((4, 2)),
-            dma((4,)), dma((4,)),
+            dma((3 + PIECES,)), dma((3 + PIECES,)),
             dma((4, 2)), dma((4, 2)),
             dma((NZD,)), dma((NZD,)),
-            dma((1,)), dma((1,)),
+            dma((2,)), dma((2,)),
+            dma((NZD,)), dma((NZD,)),
+            dma,
         ],
         compiler_params=pltpu.CompilerParams(
             collective_id=0, has_side_effects=True, vmem_limit_bytes=56 * 2**20
@@ -389,6 +431,7 @@
             flops=11 * 10**9, bytes_accessed=3 * 2**20, transcendentals=2**23
         ),
     )(queries, keys, values, attn, cotangent, out_weight, lse)
+    return (mine * 0.125 + returned.astype(F32)).astype(BF), key_grad, value_grad
 
 
 def solution(mesh):

time: 54.2 us -> 53.2 us (0.982)
  the two profiles are of different devices: /device:TPU:8 before, /device:TPU:2 now
where the time goes in v4:
time: 53.2 us; the launch traced here: 53 us
  Pallas kernels  49.1 us (92%)
  other arithmetic  1.9 us (4%)
  local copies, waits for them, and re-layouts  1.33 us (2%)
  between operations  0.65 us (1%)
    pallas_call x1, Pallas kernels, body(): pl.pallas_call(kernel, out_shape=[jax.ShapeDtypeStruct((ROWS, WIDTH), F32...  49.1 us
    convert_element_type x1, other arithmetic, body(): (mine * 0.125 + returned.astype(F32)).astype(BF)  1.9 us
    unnamed x6, local copies, waits for them, and re-layouts  1.33 us

profile of v4, /device:TPU:2, one launch (start us, length us, event | category | flops | bytes accessed | tf_op | source)
XLA Modules:
  0.0 53.0 jit_solution(11689008154608902047)
XLA Ops:
  0.6 49.1 %shard_map.94 = (f32[1024,128]{1,0:T(8,128)}, bf16[1024,128]{1,0:T(8,128)(2,1)}, bf16[64,128]{1,0:T(8,128)(2,1)}, bf16[64,128]{1,0:T(8,128)(2,1)}) custom-call(bf16[1024,128]{1,0:T(8,128)(2,1)} %q_in.1, bf16[64,128]{1,0:T(8,128)(2,1)} %k_in.1, bf16[64,128]{1,0:T(8,128)(2,1)} %v_in.1, bf16[1024,128]{1,0:T(8,128)(2,1)} %attn_in.1, bf16[1024,128]{1,0:T(8,128)(2,1)} %cot_in.1, ...), custom_call_target="tpu_custom_call" | custom-call | flops 11000000512 | bytes 3145728 | tf_op jit(solution)/shard_map/pallas_call | solution.py:378
  49.8 0.0 copy-start.1
  49.8 1.9 %add_convert_fusion = bf16[1024,128]{1,0:T(8,128)(2,1)} fusion(bf16[1024,128]{1,0:T(8,128)(2,1)} %get-tuple-element.8, f32[1024,128]{1,0:T(8,128)} %get-tuple-element.7), kind=kLoop, calls=%fused_computation | loop fusion | flops 524288 | bytes 1048576 | tf_op jit(solution)/shard_map/convert_element_type | solution.py:434
  51.7 0.0 copy-done.1
  51.7 0.0 copy-start
  51.7 0.6 %copy.12 = bf16[64,128]{1,0:T(8,128)(2,1)} copy(bf16[64,128]{1,0:T(8,128)(2,1)S(1)} %copy-done.1) | data formatting | bytes 32768
  52.3 0.1 copy-done
  52.4 0.6 %copy.13 = bf16[64,128]{1,0:T(8,128)(2,1)} copy(bf16[64,128]{1,0:T(8,128)(2,1)S(1)} %copy-done) | data formatting | bytes 32768
Async XLA Ops:
  49.8 1.9 %copy-start.1 = (bf16[64,128]{1,0:T(8,128)(2,1)S(1)}, bf16[64,128]{1,0:T(8,128)(2,1)}, u32[]{:S(2)}) copy-start(bf16[64,128]{1,0:T(8,128)(2,1)} %get-tuple-element.15) | copy-start | bytes 49156
  51.7 0.7 %copy-start = (bf16[64,128]{1,0:T(8,128)(2,1)S(1)}, bf16[64,128]{1,0:T(8,128)(2,1)}, u32[]{:S(2)}) copy-start(bf16[64,128]{1,0:T(8,128)(2,1)} %get-tuple-element.16) | copy-start | bytes 49156

commit v5 on v4

--- a/solution.py
+++ b/solution.py
@@ -350,6 +350,13 @@
     out = pltpu.make_async_copy(dq.at[0], mine_out, out_sem)
     out.start()
     gather(NEAR)
+    for c in (
+        *across, beside, *onward, *along_z.values(), swap_q, swap_l, swap_d, *swap_a,
+        *back_z2.values(), across_y,
+        *(along_y(k, p) for k in (1, 2, 3) for p in (FAR, NEAR)),
+        *(back_y(k, p) for k in (1, 3) for p in (FAR, NEAR)),
+    ):
+        c.wait_send()
     total = owned[...]
     across_y.wait_recv()
     total = total + recv2[...].astype(F32)
@@ -362,12 +369,7 @@
         c.wait_recv()
     out.wait()
 
-    for c in (
-        *across, beside, *onward, *along_z.values(), swap_q, swap_l, swap_d, *swap_a,
-        *back_z.values(), *back_z2.values(), across_y, *back_q,
-        *(along_y(k, p) for k in (1, 2, 3) for p in (FAR, NEAR)),
-        *(back_y(k, p) for k in (1, 3) for p in (FAR, NEAR)),
-    ):
+    for c in (*back_z.values(), *back_q):
         c.wait_send()
 
 

time: 53.2 us -> 53.1 us (level)
  no operation moved by 1% of the time
where the time goes in v5:
time: 53.1 us; the launch traced here: 52.9 us
  Pallas kernels  49 us (92%)
  other arithmetic  1.9 us (4%)
  local copies, waits for them, and re-layouts  1.33 us (3%)
  between operations  0.65 us (1%)
    pallas_call x1, Pallas kernels, body(): pl.pallas_call(kernel, out_shape=[jax.ShapeDtypeStruct((ROWS, WIDTH), F32...  49 us
    convert_element_type x1, other arithmetic, body(): (mine * 0.125 + returned.astype(F32)).astype(BF)  1.9 us
    unnamed x6, local copies, waits for them, and re-layouts  1.33 us

profile of v5, /device:TPU:2, one launch (start us, length us, event | category | flops | bytes accessed | tf_op | source)
XLA Modules:
  0.0 52.9 jit_solution(4789512968617033702)
XLA Ops:
  0.6 49.0 %shard_map.94 = (f32[1024,128]{1,0:T(8,128)}, bf16[1024,128]{1,0:T(8,128)(2,1)}, bf16[64,128]{1,0:T(8,128)(2,1)}, bf16[64,128]{1,0:T(8,128)(2,1)}) custom-call(bf16[1024,128]{1,0:T(8,128)(2,1)} %q_in.1, bf16[64,128]{1,0:T(8,128)(2,1)} %k_in.1, bf16[64,128]{1,0:T(8,128)(2,1)} %v_in.1, bf16[1024,128]{1,0:T(8,128)(2,1)} %attn_in.1, bf16[1024,128]{1,0:T(8,128)(2,1)} %cot_in.1, ...), custom_call_target="tpu_custom_call" | custom-call | flops 11000000512 | bytes 3145728 | tf_op jit(solution)/shard_map/pallas_call | solution.py:380
  49.7 0.0 copy-start.1
  49.7 1.9 %add_convert_fusion = bf16[1024,128]{1,0:T(8,128)(2,1)} fusion(bf16[1024,128]{1,0:T(8,128)(2,1)} %get-tuple-element.8, f32[1024,128]{1,0:T(8,128)} %get-tuple-element.7), kind=kLoop, calls=%fused_computation | loop fusion | flops 524288 | bytes 1048576 | tf_op jit(solution)/shard_map/convert_element_type | solution.py:436
  51.6 0.0 copy-done.1
  51.6 0.0 copy-start
  51.6 0.6 %copy.12 = bf16[64,128]{1,0:T(8,128)(2,1)} copy(bf16[64,128]{1,0:T(8,128)(2,1)S(1)} %copy-done.1) | data formatting | bytes 32768
  52.2 0.1 copy-done
  52.3 0.6 %copy.13 = bf16[64,128]{1,0:T(8,128)(2,1)} copy(bf16[64,128]{1,0:T(8,128)(2,1)S(1)} %copy-done) | data formatting | bytes 32768
Async XLA Ops:
  49.7 1.9 %copy-start.1 = (bf16[64,128]{1,0:T(8,128)(2,1)S(1)}, bf16[64,128]{1,0:T(8,128)(2,1)}, u32[]{:S(2)}) copy-start(bf16[64,128]{1,0:T(8,128)(2,1)} %get-tuple-element.15) | copy-start | bytes 49156
  51.6 0.7 %copy-start = (bf16[64,128]{1,0:T(8,128)(2,1)S(1)}, bf16[64,128]{1,0:T(8,128)(2,1)}, u32[]{:S(2)}) copy-start(bf16[64,128]{1,0:T(8,128)(2,1)} %get-tuple-element.16) | copy-start | bytes 49156
